TPU v7x, 256 devices: a whole 4x4x8 slice. The times are simulated.
256 devices in a mesh: dp: 64 (over z, y, core), mp: 4 (over x).
Axes of the slice: x: 4, y: 4, z: 8, core: 2. Of those that a mesh axis runs over, the one named last changes fastest.
Arguments:
- queries: bfloat16 [32768, 8192], P('dp', 'mp'), may hold values from -64 to 64
- comp_keys: bfloat16 [32768, 1024], P('dp', 'mp'), may hold values from -12 to 12
- comp_values: bfloat16 [32768, 1024], P('dp', 'mp'), may hold values from -6 to 6
- prefix_keys: bfloat16 [131072, 1024], P(('dp', 'mp')), may hold values from -6 to 6
- prefix_values: bfloat16 [131072, 1024], P(('dp', 'mp')), may hold values from -6 to 6
- prompt_of: int32 [2048, 1], P('dp'), may hold values from 0 to 63; in each aligned block of 32 rows (0 to 31, 32 to 63, ...) no two rows name the same one
Outputs:
- attended: bfloat16 [32768, 8192], P('dp', 'mp')
Inputs may be any that keep to these rules, and one draw needn't show every extreme that they name: `prompt_of`: among the 32 completions of one device, at most 1 name the same prompt.
All inputs are finite; a program needn't handle non-finite values.
Results may differ from a plain program's by a relative error of at most 0.0051.
Values may be sent and summed in bfloat16 or wider, within the bound.
A program may use at most 128 MiB of HBM per device.

v0:
```python
import math

import jax
import jax.numpy as jnp
from jax import lax
from jax.sharding import PartitionSpec as P

HD = 128
LEN = 16


def attend_prefix(query_block, cache_keys, cache_values):
    scores = jnp.einsum(
        "bnlkgd,bpkd->bnlkgp", query_block, cache_keys, preferred_element_type=jnp.float32
    ) * (1.0 / math.sqrt(query_block.shape[-1]))
    ceiling = jnp.max(scores, axis=-1, keepdims=True)
    weights = jnp.exp(scores - ceiling)
    totals = jnp.sum(weights, axis=-1, keepdims=True)
    mixed_sum = jnp.einsum(
        "bnlkgp,bpkd->bnlkgd",
        weights.astype(jnp.bfloat16),
        cache_values,
        preferred_element_type=jnp.float32,
    )
    return ((mixed_sum / totals).astype(jnp.bfloat16), ceiling[..., 0] + jnp.log(totals[..., 0]))


def attend_own(query_block, own_keys, own_values):
    length = query_block.shape[1]
    scores = jnp.einsum(
        "clkgd,cmkd->clkgm", query_block, own_keys, preferred_element_type=jnp.float32
    ) * (1.0 / math.sqrt(query_block.shape[-1]))
    causal = (jnp.arange(length)[:, None] >= jnp.arange(length)[None, :])[None, :, None, None, :]
    scores = jnp.where(causal, scores, -1e30)
    ceiling = jnp.max(scores, axis=-1, keepdims=True)
    weights = jnp.exp(scores - ceiling)
    totals = jnp.sum(weights, axis=-1, keepdims=True)
    mixed_sum = jnp.einsum(
        "clkgm,cmkd->clkgd",
        weights.astype(jnp.bfloat16),
        own_values,
        preferred_element_type=jnp.float32,
    )
    return (mixed_sum / totals, ceiling[..., 0] + jnp.log(totals[..., 0]))


def body(queries, comp_keys, comp_values, prefix_keys, prefix_values, prompt_of):
    members = lax.axis_size("dp")
    completions = prompt_of.shape[0]
    kv_width = comp_keys.shape[1]
    kv_heads = kv_width // HD
    group_size = queries.shape[1] // kv_width
    capacity = max(1, 2 * completions // members)
    slot_total = members * capacity
    cache_keys, cache_values = (
        lax.all_to_all(prefix_keys, "mp", split_axis=1, concat_axis=0, tiled=True),
        lax.all_to_all(prefix_values, "mp", split_axis=1, concat_axis=0, tiled=True),
    )
    cache_keys = cache_keys.reshape(1, -1, kv_heads, HD)
    cache_values = cache_values.reshape(1, -1, kv_heads, HD)
    routing = lax.all_gather(prompt_of, "dp", axis=0, tiled=True).reshape(members, completions)
    earlier = jnp.arange(completions)[None, :] < jnp.arange(completions)[:, None]
    same_prompt = routing[:, :, None] == routing[:, None, :]
    rank_all = jnp.sum((same_prompt & earlier[None]).astype(jnp.int32), axis=2)
    slot_all = routing * capacity + rank_all
    myself = lax.axis_index("dp")
    my_slots = lax.dynamic_index_in_dim(slot_all, myself, 0, keepdims=False)
    query_blocks = queries.reshape(completions, LEN, kv_heads, group_size, HD)
    hot_all = jnp.zeros(routing.shape, dtype=bool)
    sent_mine = jnp.logical_not(lax.dynamic_index_in_dim(hot_all, myself, 0, keepdims=False))
    chosen = (my_slots[:, None] == jnp.arange(slot_total)[None, :]) & sent_mine[:, None]
    source = jnp.sum(chosen.astype(jnp.int32) * jnp.arange(completions)[:, None], axis=0)
    filled = jnp.any(chosen, axis=0)
    outgoing = jnp.where(
        filled[:, None, None],
        queries.reshape(completions, LEN, -1)[source],
        jnp.zeros((), jnp.bfloat16),
    )
    incoming = lax.all_to_all(
        outgoing.reshape(members, capacity, LEN, -1), "dp", split_axis=0, concat_axis=0, tiled=True
    )
    arrivals = incoming.reshape(slot_total, LEN, kv_heads, group_size, HD)
    live_slots = jnp.any(
        (routing[:, :, None] == myself)
        & (rank_all[:, :, None] == jnp.arange(capacity)[None, None, :])
        & jnp.logical_not(hot_all)[:, :, None],
        axis=1,
    ).reshape(-1)
    live_count = jnp.sum(live_slots.astype(jnp.int32))
    tile_size = max(1, 128 // LEN)
    tile_count = -(-slot_total // tile_size)
    ordering = jnp.argsort((1 - live_slots.astype(jnp.int32)) * slot_total + jnp.arange(slot_total))
    padding = tile_count * tile_size - slot_total
    ordering = jnp.concatenate([ordering, jnp.broadcast_to(ordering[-1:], (padding,))], 0)

    def visit(visit_index, carried):
        mixed_acc, lse_acc = carried
        picked = lax.dynamic_slice_in_dim(ordering, visit_index * tile_size, tile_size)
        part_mixed, part_lse = attend_prefix(arrivals[picked][None], cache_keys, cache_values)
        return (mixed_acc.at[picked].set(part_mixed[0]), lse_acc.at[picked].set(part_lse[0]))

    initial = (
        jnp.zeros((slot_total, LEN, kv_heads, group_size, HD), jnp.bfloat16),
        jnp.zeros((slot_total, LEN, kv_heads, group_size), jnp.float32),
    )
    mixed_acc, lse_acc = lax.fori_loop(0, (live_count + tile_size - 1) // tile_size, visit, initial)
    own_mixed, own_lse = attend_own(
        query_blocks,
        comp_keys.reshape(completions, LEN, kv_heads, HD),
        comp_values.reshape(completions, LEN, kv_heads, HD),
    )
    returned = lax.all_to_all(
        mixed_acc.reshape(members, capacity, LEN, -1), "dp", split_axis=0, concat_axis=0, tiled=True
    )
    returned_lse = lax.all_to_all(
        lse_acc.reshape(members, capacity, LEN, -1), "dp", split_axis=0, concat_axis=0, tiled=True
    )
    prefix_mixed = returned.reshape(slot_total, LEN, kv_heads, group_size, HD)[my_slots]
    prefix_lse = returned_lse.reshape(slot_total, LEN, kv_heads, group_size)[my_slots]
    ceiling = jnp.maximum(prefix_lse, own_lse)
    far_weight = jnp.exp(prefix_lse - ceiling)
    near_weight = jnp.exp(own_lse - ceiling)
    blended = (
        prefix_mixed.astype(jnp.float32) * far_weight[..., None]
        + own_mixed * near_weight[..., None]
    ) / (far_weight + near_weight)[..., None]
    return blended.astype(jnp.bfloat16).reshape(completions * LEN, -1)


def solution(mesh):
    placed = (
        P("dp", "mp"),
        P("dp", "mp"),
        P("dp", "mp"),
        P(("dp", "mp"), None),
        P(("dp", "mp"), None),
        P("dp", None),
    )
    return jax.shard_map(body, mesh=mesh, in_specs=placed, out_specs=P("dp", "mp"), check_vma=False)
```

profile of v0, /device:TPU:1, one launch (start us, length us, event | category | flops | bytes accessed | tf_op | source)
XLA Modules:
  0.0 475.4 jit_solution(1708341922271124918)
XLA Ops:
  0.0 2.4 copy.197
  2.4 4.8 %all-to-all-start.1 = ((bf16[512,4,256]{2,0,1:T(8,128)(2,1)}), bf16[512,4,256]{2,0,1:T(8,128)(2,1)S(1)}, u32[]{:S(2)}, u32[]{:S(2)}) async-start(bf16[512,4,256]{2,0,1:T(8,128)(2,1)} %bitcast.161), calls=%async_computation.1 | async-start | bytes 2097152 | tf_op jit(solution)/shard_map/all_to_all | solution.py:56
  7.3 0.7 dynamic-slice
  8.8 21.3 %all-reduce = s32[2048]{0:T(1024)S(1)} all-reduce(s32[2048]{0:T(1024)S(1)} %bitcast_dynamic-update-slice_fusion), channel_id=1, replica_groups=mesh['dp'=64,'mp'=4] {'dp'}, use_global_device_ids=true, to_apply=%add | all-reduce | flops 2048 | bytes 16384
  30.2 2.3 copy.196
  33.1 4.3 all-to-all-start.2
  37.4 2.8 gather_fusion.1
  40.2 4.5 bitcast_select_fusion.1
  44.7 2.9 all-to-all-done.2
  47.7 10.8 %all-to-all-start = ((bf16[64,1,16,2048]{3,2,1,0:T(8,128)(2,1)}), bf16[64,1,16,2048]{3,2,1,0:T(8,128)(2,1)}, u32[]{:S(2)}, u32[]{:S(2)}) async-start(bf16[64,1,16,2048]{3,2,1,0:T(8,128)(2,1)} %bitcast_select_fusion.1), calls=%async_computation | async-start | bytes 8388608 | tf_op jit(solution)/shard_map/all_to_all | solution.py:79
  58.7 0.6 iota_add_fusion
  60.0 2.1 sort.17
  62.5 1.3 reshape.221
  64.0 89.1 %all-to-all-done = bf16[64,1,16,2048]{3,2,1,0:T(8,128)(2,1)} async-done(((bf16[64,1,16,2048]{3,2,1,0:T(8,128)(2,1)}), bf16[64,1,16,2048]{3,2,1,0:T(8,128)(2,1)}, u32[]{:S(2)}, u32[]{:S(2)}) %all-to-all-start) | async-done | bytes 4194336 | tf_op jit(solution)/shard_map/all_to_all | solution.py:79
  153.1 5.5 %copy.176 = bf16[128,8,16,128]{3,2,1,0:T(8,128)(2,1)} copy(bf16[128,8,16,128]{3,1,2,0:T(8,128)(2,1)} %bitcast.45) | data formatting | bytes 8388608
  158.7 3.0 broadcast_in_dim.26
  161.7 86.8 %while.12 = (s32[]{:T(128)}, bf16[64,16,2,8,128]{4,3,2,1,0:T(8,128)(2,1)}, f32[64,16,2,8]{1,3,2,0:T(8,128)S(1)}, s32[]{:T(128)}, s32[64]{0:T(128)S(1)}, /*index=...) while((s32[]{:T(128)}, ...), condition=%wide.region_11.12_spmd, body=%wide.region_6.11_spmd.sunk | while | flops 2181561344 | bytes 124367232 | solution.py:106
  161.8 2.8 gather_fusion
  164.6 2.4 bitcast_reduce_fusion.2
  167.1 3.3 fusion.51
  170.4 2.4 copy-done
  172.9 0.7 scatter_fusion.1
  173.6 7.2 %fusion.52 = bf16[8,16,2,8,128]{4,3,1,0,2:T(8,128)(2,1)S(1)} fusion(f32[2,8,16,8,2048]{4,3,2,1,0:T(8,128)} %copy-done, f32[8,16,2,8]{3,1,0,2:T(8,128)S(1)} %get-tuple-element.189, bf16[1,2048,2,128]{3,1,2,0:T(8,128)(2,1)S(1)} %get-tuple-element.221, f32[8,16,2,8]{3,1,0,2:T(8,128)S(1)} %fusion.51), kind=kOutput, calls=%fused_computation.16.clone.1 | convolution fusion | flops 1086849024 | bytes 18366464 | tf_op jit(solution)/shard_map/while/body/bnlkgp,bpkd->bnlkgd/dot_general | solution.py:19
  180.9 2.5 scatter_fusion
  183.5 2.8 gather_fusion
  186.3 2.4 bitcast_reduce_fusion.2
  188.8 3.3 fusion.51
  192.1 2.4 copy-done
  194.6 0.7 scatter_fusion.1
  195.3 7.2 %fusion.52 = bf16[8,16,2,8,128]{4,3,1,0,2:T(8,128)(2,1)S(1)} fusion(f32[2,8,16,8,2048]{4,3,2,1,0:T(8,128)} %copy-done, f32[8,16,2,8]{3,1,0,2:T(8,128)S(1)} %get-tuple-element.189, bf16[1,2048,2,128]{3,1,2,0:T(8,128)(2,1)S(1)} %get-tuple-element.221, f32[8,16,2,8]{3,1,0,2:T(8,128)S(1)} %fusion.51), kind=kOutput, calls=%fused_computation.16.clone.1 | convolution fusion | flops 1086849024 | bytes 18366464 | tf_op jit(solution)/shard_map/while/body/bnlkgp,bpkd->bnlkgd/dot_general | solution.py:19
  202.6 2.5 scatter_fusion
  205.2 2.8 gather_fusion
  208.1 2.4 bitcast_reduce_fusion.2
  210.5 3.3 fusion.51
  213.8 2.4 copy-done
  216.3 0.7 scatter_fusion.1
  217.1 7.2 %fusion.52 = bf16[8,16,2,8,128]{4,3,1,0,2:T(8,128)(2,1)S(1)} fusion(f32[2,8,16,8,2048]{4,3,2,1,0:T(8,128)} %copy-done, f32[8,16,2,8]{3,1,0,2:T(8,128)S(1)} %get-tuple-element.189, bf16[1,2048,2,128]{3,1,2,0:T(8,128)(2,1)S(1)} %get-tuple-element.221, f32[8,16,2,8]{3,1,0,2:T(8,128)S(1)} %fusion.51), kind=kOutput, calls=%fused_computation.16.clone.1 | convolution fusion | flops 1086849024 | bytes 18366464 | tf_op jit(solution)/shard_map/while/body/bnlkgp,bpkd->bnlkgd/dot_general | solution.py:19
  224.4 2.5 scatter_fusion
  226.9 2.8 gather_fusion
  229.8 2.4 bitcast_reduce_fusion.2
  232.2 3.3 fusion.51
  235.5 2.4 copy-done
  238.0 0.7 scatter_fusion.1
  238.8 7.2 %fusion.52 = bf16[8,16,2,8,128]{4,3,1,0,2:T(8,128)(2,1)S(1)} fusion(f32[2,8,16,8,2048]{4,3,2,1,0:T(8,128)} %copy-done, f32[8,16,2,8]{3,1,0,2:T(8,128)S(1)} %get-tuple-element.189, bf16[1,2048,2,128]{3,1,2,0:T(8,128)(2,1)S(1)} %get-tuple-element.221, f32[8,16,2,8]{3,1,0,2:T(8,128)S(1)} %fusion.51), kind=kOutput, calls=%fused_computation.16.clone.1 | convolution fusion | flops 1086849024 | bytes 18366464 | tf_op jit(solution)/shard_map/while/body/bnlkgp,bpkd->bnlkgd/dot_general | solution.py:19
  246.1 2.5 scatter_fusion
  248.6 0.9 reshape.296
  249.4 93.6 %all-to-all-start.4 = ((f32[64,1,256]{2,1,0:T(1,128)}), f32[64,1,256]{2,1,0:T(1,128)S(1)}, u32[]{:S(2)}, u32[]{:S(2)}) async-start(f32[64,1,256]{2,1,0:T(1,128)} %reshape.296), calls=%async_computation.4 | async-start | bytes 131072 | tf_op jit(solution)/shard_map/all_to_all | solution.py:115
  343.1 7.3 %reshape.222 = bf16[64,1,16,2048]{3,2,1,0:T(8,128)(2,1)} reshape(bf16[64,16,2,8,128]{4,3,2,1,0:T(8,128)(2,1)} %get-tuple-element.51) | data formatting | bytes 8388608 | tf_op jit(solution)/shard_map/reshape | solution.py:113
  350.4 2.8 all-to-all-done.4
  353.1 7.8 %all-to-all-start.3 = ((bf16[64,1,16,2048]{3,2,1,0:T(8,128)(2,1)}), bf16[64,1,16,2048]{3,2,1,0:T(8,128)(2,1)}, u32[]{:S(2)}, u32[]{:S(2)}) async-start(bf16[64,1,16,2048]{3,2,1,0:T(8,128)(2,1)} %reshape.222), calls=%async_computation.3 | async-start | bytes 8388608 | tf_op jit(solution)/shard_map/all_to_all | solution.py:112
  361.0 1.9 copy.178
  363.0 8.6 %fusion.29 = (f32[32,16,2,8]{1,3,2,0:T(8,128)S(1)}, f32[32,2,16,16,8]{3,2,4,1,0:T(8,128)}) fusion(pred[16,16]{0,1:T(8,128)(4,1)S(1)} %iota_compare_fusion.2, bf16[32,16,2,8,128]{4,3,2,1,0:T(8,128)(2,1)} %bitcast.159, bf16[32,16,2,128,1]{3,2,1,0,4:T(2,128)(2,1)S(1)} %bitcast.163), kind=kOutput, calls=%fused_computation.35 | convolution fusion | flops 33939456 | bytes 2916608 | tf_op jit(solution)/shard_map/clkgd,cmkd->clkgm/dot_general | solution.py:30
  371.8 4.0 fusion.28
  376.0 1.1 copy.162
  377.1 3.1 copy.160
  380.3 0.5 broadcast.160
  380.8 0.8 reduce.6
  381.9 0.6 gather_fusion.3
  383.7 1.3 copy.164
  385.0 70.4 %all-to-all-done.3 = bf16[64,1,16,2048]{3,2,1,0:T(8,128)(2,1)} async-done(((bf16[64,1,16,2048]{3,2,1,0:T(8,128)(2,1)}), bf16[64,1,16,2048]{3,2,1,0:T(8,128)(2,1)}, u32[]{:S(2)}, u32[]{:S(2)}) %all-to-all-start.3) | async-done | bytes 4194336 | tf_op jit(solution)/shard_map/all_to_all | solution.py:112
  455.4 5.6 %copy.177 = bf16[128,8,16,128]{3,2,1,0:T(8,128)(2,1)} copy(bf16[128,8,16,128]{3,1,2,0:T(8,128)(2,1)} %bitcast.51) | data formatting | bytes 8388608
  461.0 4.5 gather_fusion.2
  465.5 7.3 %fusion.26 = bf16[32,16,2,8,128]{4,3,1,2,0:T(8,128)(2,1)S(1)} fusion(bf16[32,16,2,8,16]{4,3,1,2,0:T(8,128)(2,1)S(1)} %copy-done.3, bf16[32,16,2,8,128]{4,3,2,1,0:T(8,128)(2,1)} %gather_fusion.2, f32[32,16,2,8]{3,1,2,0:T(8,128)} %copy.164, f32[32,16,2,8]{3,1,2,0:T(8,128)S(1)} %copy.163, f32[32,16,2,8]{3,1,2,0:T(8,128)} %copy.162, ...), kind=kOutput, calls=%fused_computation.32 | convolution fusion | flops 40894464 | bytes 4849664 | tf_op jit(solution)/shard_map/clkgm,cmkd->clkgd/dot_general | solution.py:38
  473.1 2.3 reshape.229
  (74 shorter events, 5.2 us)
Async XLA Ops:
  0.0 7.3 %copy-start.7 = (u32[256]{0:T(256)S(1)}, u32[256]{0:T(256)}, u32[]{:S(2)}) copy-start(u32[256]{0:T(256)} %constant.79) | copy-start | bytes 3076
  0.0 8.6 %copy-start.6 = (s32[32,1]{0,1:T(1,128)S(1)}, s32[32,1]{0,1:T(1,128)}, u32[]{:S(2)}) copy-start(s32[32,1]{0,1:T(1,128)} %param.13) | copy-start | bytes 388
  0.0 37.3 %copy-start.1 = (bf16[512,2048]{1,0:T(8,128)(2,1)S(1)}, bf16[512,2048]{1,0:T(8,128)(2,1)}, u32[]{:S(2)}) copy-start(bf16[512,2048]{1,0:T(8,128)(2,1)} %param.8) | copy-start | bytes 6291460
  2.4 30.6 %all-to-all-start.1 = ((bf16[512,4,256]{2,0,1:T(8,128)(2,1)}), bf16[512,4,256]{2,0,1:T(8,128)(2,1)S(1)}, u32[]{:S(2)}, u32[]{:S(2)}) async-start(bf16[512,4,256]{2,0,1:T(8,128)(2,1)} %bitcast.161), calls=%async_computation.1 | async-start | bytes 2097152 | tf_op jit(solution)/shard_map/all_to_all | solution.py:56
  33.1 14.6 %all-to-all-start.2 = ((bf16[512,4,256]{2,0,1:T(8,128)(2,1)}), bf16[512,4,256]{2,0,1:T(8,128)(2,1)}, u32[]{:S(2)}, u32[]{:S(2)}) async-start(bf16[512,4,256]{2,0,1:T(8,128)(2,1)} %bitcast.162), calls=%async_computation.2 | async-start | bytes 2097152 | tf_op jit(solution)/shard_map/all_to_all | solution.py:57
  47.7 105.5 %all-to-all-start = ((bf16[64,1,16,2048]{3,2,1,0:T(8,128)(2,1)}), bf16[64,1,16,2048]{3,2,1,0:T(8,128)(2,1)}, u32[]{:S(2)}, u32[]{:S(2)}) async-start(bf16[64,1,16,2048]{3,2,1,0:T(8,128)(2,1)} %bitcast_select_fusion.1), calls=%async_computation | async-start | bytes 8388608 | tf_op jit(solution)/shard_map/all_to_all | solution.py:79
  167.1 5.7 %copy-start = (f32[2,8,16,8,2048]{4,3,2,1,0:T(8,128)}, f32[2,8,16,8,2048]{4,3,2,1,0:T(8,128)S(1)}, u32[]{:S(2)}) copy-start(f32[2,8,16,8,2048]{4,3,2,1,0:T(8,128)S(1)} %get-tuple-element.188) | copy-start | bytes 50331652 | tf_op jit(solution)/shard_map/while
  188.8 5.7 %copy-start = (f32[2,8,16,8,2048]{4,3,2,1,0:T(8,128)}, f32[2,8,16,8,2048]{4,3,2,1,0:T(8,128)S(1)}, u32[]{:S(2)}) copy-start(f32[2,8,16,8,2048]{4,3,2,1,0:T(8,128)S(1)} %get-tuple-element.188) | copy-start | bytes 50331652 | tf_op jit(solution)/shard_map/while
  210.5 5.7 %copy-start = (f32[2,8,16,8,2048]{4,3,2,1,0:T(8,128)}, f32[2,8,16,8,2048]{4,3,2,1,0:T(8,128)S(1)}, u32[]{:S(2)}) copy-start(f32[2,8,16,8,2048]{4,3,2,1,0:T(8,128)S(1)} %get-tuple-element.188) | copy-start | bytes 50331652 | tf_op jit(solution)/shard_map/while
  232.2 5.7 %copy-start = (f32[2,8,16,8,2048]{4,3,2,1,0:T(8,128)}, f32[2,8,16,8,2048]{4,3,2,1,0:T(8,128)S(1)}, u32[]{:S(2)}) copy-start(f32[2,8,16,8,2048]{4,3,2,1,0:T(8,128)S(1)} %get-tuple-element.188) | copy-start | bytes 50331652 | tf_op jit(solution)/shard_map/while
  249.4 103.7 %all-to-all-start.4 = ((f32[64,1,256]{2,1,0:T(1,128)}), f32[64,1,256]{2,1,0:T(1,128)S(1)}, u32[]{:S(2)}, u32[]{:S(2)}) async-start(f32[64,1,256]{2,1,0:T(1,128)} %reshape.296), calls=%async_computation.4 | async-start | bytes 131072 | tf_op jit(solution)/shard_map/all_to_all | solution.py:115
  350.4 10.6 %copy-start.2 = (bf16[512,2048]{1,0:T(8,128)(2,1)S(1)}, bf16[512,2048]{1,0:T(8,128)(2,1)}, u32[]{:S(2)}) copy-start(bf16[512,2048]{1,0:T(8,128)(2,1)} %param.8) | copy-start | bytes 6291460
  353.1 102.3 %all-to-all-start.3 = ((bf16[64,1,16,2048]{3,2,1,0:T(8,128)(2,1)}), bf16[64,1,16,2048]{3,2,1,0:T(8,128)(2,1)}, u32[]{:S(2)}, u32[]{:S(2)}) async-start(bf16[64,1,16,2048]{3,2,1,0:T(8,128)(2,1)} %reshape.222), calls=%async_computation.3 | async-start | bytes 8388608 | tf_op jit(solution)/shard_map/all_to_all | solution.py:112
  361.0 2.0 copy-start.4
  375.9 4.3 copy-start.5
  461.0 4.5 copy-start.3
where the time goes:
time: 478 us; the launch traced here: 475 us
  waiting for transfers between devices  165 us (35%)
  starting transfers between devices  121 us (25%)
  local copies, waits for them, and re-layouts  84.7 us (18%)
  matrix products  54.4 us (11%)
  other arithmetic  26.5 us (6%)
  blocking collectives  21.3 us (4%)
    all_to_all x1, starting transfers between devices, body(): lax.all_to_all(lse_acc.reshape(members, capacity, LEN, -1), 'dp', split_a...  93.6 us
    all_to_all x1, waiting for transfers between devices, body(): lax.all_to_all(outgoing.reshape(members, capacity, LEN, -1), 'dp', split_...  89.1 us
    all_to_all x1, waiting for transfers between devices, body(): lax.all_to_all(mixed_acc.reshape(members, capacity, LEN, -1), 'dp', split...  70.4 us
    dot_general x4, matrix products, attend_prefix(): jnp.einsum('bnlkgp,bpkd->bnlkgd', weights.astype(jnp.bfloat16), cache_val...  28.8 us
    unnamed x1, blocking collectives  21.3 us
    unnamed x23, local copies, waits for them, and re-layouts  14.9 us
    reduce_sum x4, other arithmetic, attend_prefix(): totals = jnp.sum(weights, axis=-1, keepdims=True)  13.3 us
    gather x4, local copies, waits for them, and re-layouts, visit(): arrivals[picked][None]  11.3 us
  transfers between devices with their start and end apart: 5, of which 4 were waited for; matrix products, arithmetic and copies ran while one was open for 10% of the time, Pallas kernels for 0%

commit v1 on v0

v1 whole, which is shorter than its diff:
```python
import functools
import math

import jax
import jax.numpy as jnp
from jax import lax
from jax.experimental import pallas as pl
from jax.experimental.pallas import tpu as pltpu
from jax.sharding import PartitionSpec as P

MESH = pl.DeviceIdType.MESH
HD = 128
LEN = 16
GROUP = 8
HEADS = 2
PLANE = 8
RING = 8
SLOT = GROUP * HD
WIDE = SLOT + HD
SCALE = 1.0 / math.sqrt(HD)
LOG2E = math.log2(math.e)
ORDER = (0, 1, 7, 2, 6, 3, 5, 4)


def split3(x):
    hi = x.astype(jnp.bfloat16)
    rest = x - hi.astype(jnp.float32)
    mid = rest.astype(jnp.bfloat16)
    low = (rest - mid.astype(jnp.float32)).astype(jnp.bfloat16)
    return hi, mid, low


def by_group(column):
    lane = lax.broadcasted_iota(jnp.int32, (LEN, HD), 1)
    out = jnp.zeros((LEN, HD), jnp.float32)
    for g in range(GROUP):
        out = jnp.where(lane == g, column[g * LEN : (g + 1) * LEN], out)
    return out


def rows_of(slot):
    return [slot[:, g * HD : (g + 1) * HD] for g in range(GROUP)]


def kernel(
    idx, pos, q, ck, cv, pk, pv, out,
    cache, qs, fs, nq, relay_q, fq, no, fo, relay_o, ret, own, own_lse,
    send_sem, recv_sem, local_sem,
):
    dp, x = lax.axis_index("dp"), lax.axis_index("mp")
    z, lane = dp // PLANE, dp % PLANE
    xs = lax.axis_size("mp")
    share = pk.shape[0]
    comps = q.shape[0]

    def to_x(e):
        return (dp, (x + e) % xs)

    def to_z(k):
        return (((z + k + RING) % RING) * PLANE + lane, x)

    def to_lane(d):
        return (z * PLANE + (lane + d + PLANE) % PLANE, x)

    barrier = pltpu.get_barrier_semaphore()
    friends = (
        [to_x(e) for e in range(1, xs)]
        + [to_z(k) for k in (1, -1, 2, -2)]
        + [to_lane(d) for d in range(1, PLANE)]
    )
    for friend in friends:
        pl.semaphore_signal(barrier, 1, device_id=friend, device_id_type=MESH)
    pl.semaphore_wait(barrier, len(friends))

    count = [0]
    sent = []

    def remote(src, dst, device):
        n = count[0]
        count[0] += 1
        copy = pltpu.make_async_remote_copy(
            src_ref=src, dst_ref=dst, send_sem=send_sem.at[n], recv_sem=recv_sem.at[n],
            device_id=device, device_id_type=MESH,
        )
        copy.start()
        sent.append(copy)
        return copy

    def columns(e, h):
        return pl.ds(pl.multiple_of(((x + e) % xs) * (HEADS * HD) + h * HD, HD), HD)

    def exchange(h):
        copies = []
        for w, whole in enumerate((pk, pv)):
            mine = pltpu.make_async_copy(
                whole.at[:, columns(0, h)], cache.at[0, h, w, pl.ds(0, share)],
                local_sem.at[h * 2 + w],
            )
            mine.start()
            copies.append([mine] + [
                remote(whole.at[:, columns(e, h)], cache.at[0, h, w, pl.ds(e * share, share)], to_x(e))
                for e in range(1, xs)
            ])
        return copies

    def arrive(copies):
        copies[0].wait()
        for copy in copies[1:]:
            copy.wait_recv()

    def spread(h, w, places):
        return {j: remote(cache.at[0, h, w], cache.at[j, h, w], to_z(k)) for j, k in places}

    EDGE, NEXT = ((3, -2), (4, 2)), ((1, -1), (2, 1))

    parts0 = exchange(0)

    def pack(d, first, last, dst):
        for rr in range(first, last):
            dst[rr - first] = q[idx[d * RING + rr]]

    pack(0, 5, 8, relay_q.at[0])
    for d in range(1, PLANE):
        pack(d, 5, 8, fs.at[d])
    far_y = [remote(fs.at[d], relay_q.at[d], to_lane(d)) for d in range(1, PLANE)]
    pack(0, 0, 5, nq.at[0])
    for d in range(1, PLANE):
        pack(d, 0, 5, qs.at[d])
    near_y = [remote(qs.at[d], nq.at[d], to_lane(d)) for d in range(1, PLANE)]

    spread0 = []
    for w in range(2):
        arrive(parts0[w])
        spread0.append({**spread(0, w, EDGE), **spread(0, w, NEXT)})
    parts1 = exchange(1)

    block = HD // LEN
    rows = block * HD
    r_at = lax.broadcasted_iota(jnp.int32, (rows, HD), 0)
    c_at = lax.broadcasted_iota(jnp.int32, (rows, HD), 1)
    allowed = (r_at // HD == c_at // LEN) & (r_at % LEN >= c_at % LEN)

    def own_block(b, carry):
        keys, values = ck[b], cv[b]
        for h in range(HEADS):
            pieces = []
            for c in range(block):
                pieces += rows_of(q[b * block + c, :, h * SLOT : (h + 1) * SLOT])
            part = slice(h * HD, (h + 1) * HD)
            s = lax.dot_general(
                jnp.concatenate(pieces, axis=0), keys[:, part], (((1,), (1,)), ((), ())),
                preferred_element_type=jnp.float32,
            ) * SCALE
            s = jnp.where(allowed, s, -1e30)
            top = jnp.max(s, axis=1, keepdims=True)
            w = jnp.exp(s - top)
            total = jnp.sum(w, axis=1, keepdims=True)
            mixed = jnp.dot(
                w.astype(jnp.bfloat16), values[:, part], preferred_element_type=jnp.float32
            ) / total
            lse = top + jnp.log(total)
            for c in range(block):
                for g in range(GROUP):
                    at = c * HD + g * LEN
                    own[b * block + c, :, h * SLOT + g * HD : h * SLOT + (g + 1) * HD] = (
                        mixed[at : at + LEN]
                    )
                own_lse[b * block + c, h] = by_group(lse[c * HD : (c + 1) * HD])
        return carry

    lax.fori_loop(0, comps // block, own_block, 0)

    for copy in far_y:
        copy.wait_recv()
    half = PLANE // 2
    far_q = [
        remote(relay_q.at[:, 0], fq.at[pl.ds(0, 8)], to_z(1)),
        remote(relay_q.at[:, 1], fq.at[pl.ds(12, 8)], to_z(-1)),
        remote(relay_q.at[pl.ds(0, half), 2], fq.at[pl.ds(8, half)], to_z(2)),
        remote(relay_q.at[pl.ds(half, half), 2], fq.at[pl.ds(20, half)], to_z(-2)),
    ]

    def attend(queries, j, h):
        pieces = []
        for slot in queries:
            pieces += rows_of(slot)
        s = lax.dot_general(
            jnp.concatenate(pieces, axis=0), cache[j, h, 0], (((1,), (1,)), ((), ())),
            preferred_element_type=jnp.float32,
        )
        top = jnp.max(s, axis=1, keepdims=True)
        w = jnp.exp2((s - top) * (SCALE * LOG2E))
        total = jnp.sum(w, axis=1, keepdims=True)
        mixed = jnp.dot(w.astype(jnp.bfloat16), cache[j, h, 1], preferred_element_type=jnp.float32)
        mixed = (mixed / total).astype(jnp.bfloat16)
        lse = top * SCALE + jnp.log(total)
        results = []
        for n in range(len(queries)):
            at = n * HD
            hi, mid, low = split3(by_group(lse[at : at + HD]))
            tail = jnp.concatenate(
                [hi[:, :GROUP], mid[:, :GROUP], low[:, :GROUP], hi[:, 3 * GROUP :]], axis=1
            )
            results.append(
                [mixed[at + g * LEN : at + (g + 1) * LEN] for g in range(GROUP)] + [tail]
            )
        return results

    def put(dst, i, pieces):
        for g, piece in enumerate(pieces):
            dst[i + (slice(None), slice(g * HD, (g + 1) * HD))] = piece

    def head(h):
        return slice(h * SLOT, (h + 1) * SLOT)

    def near(h, first, last):
        def step(n, carry):
            j, d = first + n // (PLANE // 2), 2 * (n % (PLANE // 2))
            two = attend([nq[d, j, :, head(h)], nq[d + 1, j, :, head(h)]], j, h)
            for k in range(2):
                put(no, (h, d + k, j), two[k])
            return carry

        lax.fori_loop(0, (last - first) * (PLANE // 2), step, 0)

    def far(h):
        def step(n, carry):
            two = attend([fq[2 * n, :, head(h)], fq[2 * n + 1, :, head(h)]], 3 + n // 6, h)
            for k in range(2):
                put(fo, (h, 2 * n + k), two[k])
            return carry

        lax.fori_loop(0, 12, step, 0)

    returned = []

    def give_near(h, first, last):
        span = pl.ds(first, last - first)
        for d in range(1, PLANE):
            returned.append(remote(no.at[h, d, span], ret.at[h, pl.ds(d * RING + first, last - first)], to_lane(-d)))
        ret[h, first:last] = no[h, 0, first:last]

    def give_far(h):
        return [
            remote(fo.at[h, pl.ds(0, 8)], relay_o.at[h, 0], to_z(-1)),
            remote(fo.at[h, pl.ds(12, 8)], relay_o.at[h, 1], to_z(1)),
            remote(fo.at[h, pl.ds(8, half)], relay_o.at[h, 2, pl.ds(0, half)], to_z(-2)),
            remote(fo.at[h, pl.ds(20, half)], relay_o.at[h, 2, pl.ds(half, half)], to_z(2)),
        ]

    def pass_far(h, copies):
        for rr in range(3):
            for copy in (copies[rr : rr + 1] if rr < 2 else copies[2:]):
                copy.wait_recv()
            for d in range(1, PLANE):
                returned.append(remote(relay_o.at[h, rr, d], ret.at[h, d * RING + 5 + rr], to_lane(-d)))
            ret[h, 5 + rr] = relay_o[h, rr, 0]

    for w in range(2):
        arrive(parts1[w])
    for copy in near_y:
        copy.wait_recv()
    near(0, 0, 1)
    near(1, 0, 1)

    for copies in spread0:
        for copy in copies.values():
            copy.wait_send()
    edge1 = [spread(1, w, EDGE) for w in range(2)]
    for copies in spread0:
        for copy in copies.values():
            copy.wait_recv()
    near(0, 1, 5)
    give_near(0, 0, 5)
    for copy in far_q:
        copy.wait_recv()
    far(0)
    back0 = give_far(0)
    next1 = [spread(1, w, NEXT) for w in range(2)]

    for copies in edge1:
        for copy in copies.values():
            copy.wait_recv()
    far(1)
    back1 = give_far(1)
    pass_far(0, back0)
    near(1, 3, 5)
    give_near(1, 3, 5)
    for copies in next1:
        for copy in copies.values():
            copy.wait_recv()
    near(1, 1, 3)
    give_near(1, 0, 3)
    pass_far(1, back1)
    for copy in returned:
        copy.wait_recv()

    def blend(c, carry):
        for h in range(HEADS):
            slot = ret[h, pos[c]]
            tail = slot[:, SLOT:].astype(jnp.float32)
            far_lse = tail[:, :GROUP] + tail[:, GROUP : 2 * GROUP] + tail[:, 2 * GROUP : 3 * GROUP]
            near_lse = own_lse[c, h][:, :GROUP]
            ceiling = jnp.maximum(far_lse, near_lse)
            a, b = jnp.exp(far_lse - ceiling), jnp.exp(near_lse - ceiling)
            inverse = 1.0 / (a + b)
            a, b = a * inverse, b * inverse
            for g in range(GROUP):
                part = slice(h * SLOT + g * HD, h * SLOT + (g + 1) * HD)
                out[c, :, part] = (
                    slot[:, g * HD : (g + 1) * HD].astype(jnp.float32) * a[:, g : g + 1]
                    + own[c, :, part] * b[:, g : g + 1]
                ).astype(jnp.bfloat16)
        return carry

    lax.fori_loop(0, comps, blend, 0)
    already = {id(copy) for copies in spread0 for copy in copies.values()}
    for copy in sent:
        if id(copy) not in already:
            copy.wait_send()


def body(queries, comp_keys, comp_values, prefix_keys, prefix_values, prompt_of):
    comps = prompt_of.shape[0]
    dp = lax.axis_index("dp")
    prompt = prompt_of[:, 0]
    distance = (prompt // PLANE - dp // PLANE) % RING
    offset = (prompt % PLANE - dp % PLANE) % PLANE
    place = jnp.zeros_like(distance)
    for n, r in enumerate(ORDER):
        place = jnp.where(distance == r, n, place)
    pos = offset * RING + place
    slots = jnp.arange(PLANE * RING)
    idx = jnp.sum(
        jnp.where(pos[None, :] == slots[:, None], jnp.arange(comps)[None, :], 0), axis=1
    ).astype(jnp.int32)
    keys = prefix_keys.shape[0] * lax.axis_size("mp")
    bf16 = jnp.bfloat16
    blocks = comp_keys.shape[0] // HD
    vmem, smem = pl.BlockSpec(memory_space=pltpu.VMEM), pl.BlockSpec(memory_space=pltpu.SMEM)
    hbm = pl.BlockSpec(memory_space=pl.ANY)
    copies = 160
    out = pl.pallas_call(
        kernel,
        out_shape=jax.ShapeDtypeStruct((comps, LEN, queries.shape[1]), bf16),
        in_specs=[smem, smem, vmem, vmem, vmem, hbm, hbm],
        out_specs=vmem,
        scratch_shapes=[
            pltpu.VMEM((5, HEADS, 2, keys, HD), bf16),
            pltpu.VMEM((PLANE, 5, LEN, HEADS * SLOT), bf16),
            pltpu.VMEM((PLANE, 3, LEN, HEADS * SLOT), bf16),
            pltpu.VMEM((PLANE, 5, LEN, HEADS * SLOT), bf16),
            pltpu.VMEM((PLANE, 3, LEN, HEADS * SLOT), bf16),
            pltpu.VMEM((24, LEN, HEADS * SLOT), bf16),
            pltpu.VMEM((HEADS, PLANE, 5, LEN, WIDE), bf16),
            pltpu.VMEM((HEADS, 24, LEN, WIDE), bf16),
            pltpu.VMEM((HEADS, 3, PLANE, LEN, WIDE), bf16),
            pltpu.VMEM((HEADS, PLANE * RING, LEN, WIDE), bf16),
            pltpu.VMEM((comps, LEN, HEADS * SLOT), jnp.float32),
            pltpu.VMEM((comps, HEADS, LEN, HD), jnp.float32),
            pltpu.SemaphoreType.DMA((copies,)),
            pltpu.SemaphoreType.DMA((copies,)),
            pltpu.SemaphoreType.DMA((4,)),
        ],
        compiler_params=pltpu.CompilerParams(
            collective_id=0, has_side_effects=True, vmem_limit_bytes=60 * 1024 * 1024
        ),
        name="attend_all",
    )(
        idx,
        pos,
        queries.reshape(comps, LEN, -1),
        comp_keys.reshape(blocks, HD, -1),
        comp_values.reshape(blocks, HD, -1),
        prefix_keys,
        prefix_values,
    )
    return out.reshape(queries.shape)


def solution(mesh):
    placed = (
        P("dp", "mp"),
        P("dp", "mp"),
        P("dp", "mp"),
        P(("dp", "mp"), None),
        P(("dp", "mp"), None),
        P("dp", None),
    )
    return jax.shard_map(body, mesh=mesh, in_specs=placed, out_specs=P("dp", "mp"), check_vma=False)
```

time: 478 us -> 237 us (0.50)
  Pallas kernels: 0 us -> 232 us
  waiting for transfers between devices: 165 us -> 0 us
  starting transfers between devices: 121 us -> 0 us
  local copies, waits for them, and re-layouts: 84.7 us -> 3.16 us
  matrix products: 54.4 us -> 0 us
  other arithmetic: 26.5 us -> 1.28 us
  blocking collectives: 21.3 us -> 0 us
    pallas_call x0 -> x1, Pallas kernels: none -> 232 us  [body(): pl.pallas_call(kernel, out_shape=jax.ShapeDtypeStruct((comps, LEN, querie...]
    all_to_all x5 -> x0, waiting for transfers between devices: 165 us -> none  [the longest x1 89.1 us: body(): lax.all_to_all(outgoing.reshape(members, capacity, LEN, -1), 'dp', split_...]
    all_to_all x5 -> x0, starting transfers between devices: 121 us -> none  [the longest x1 93.6 us: body(): lax.all_to_all(lse_acc.reshape(members, capacity, LEN, -1), 'dp', split_a...]
    dot_general x10 -> x0, matrix products: 54.4 us -> none  [the longest x4 28.8 us: attend_prefix(): jnp.einsum('bnlkgp,bpkd->bnlkgd', weights.astype(jnp.bfloat16), cache_val...]
    unnamed x1 -> x0, blocking collectives: 21.3 us -> none
    gather x8 -> x0, local copies, waits for them, and re-layouts: 19.4 us -> none  [the longest x4 11.3 us: visit(): arrivals[picked][None]]
    reduce_sum x7 -> x1, other arithmetic: 17.7 us -> 0.6 us  [body(): jnp.sum(jnp.where(pos[None, :] == slots[:, None], jnp.arange(comps)[None,...]
    scatter x8 -> x0, local copies, waits for them, and re-layouts: 12.8 us -> none  [the longest x4 9.89 us: visit(): mixed_acc.at[picked].set(part_mixed[0])]
  transfers between devices with their start and end apart: 5 -> 0, of which waited for: 4 -> 0; matrix products, arithmetic and copies ran while one was open for 10% -> 0% of each run, Pallas kernels for 0% -> 0%
where the time goes in v1:
time: 237 us
  Pallas kernels  232 us (98%)
  local copies, waits for them, and re-layouts  3.16 us (1%)
    pallas_call x1, Pallas kernels, body(): pl.pallas_call(kernel, out_shape=jax.ShapeDtypeStruct((comps, LEN, querie...  232 us

profile of v1, /device:TPU:1, one launch (start us, length us, event | category | flops | bytes accessed | tf_op | source)
XLA Modules:
  0.0 236.5 jit_solution(6013348657496290844)
XLA Ops:
  0.0 0.7 fusion.2.pos
  0.7 0.0 copy-start
  0.7 0.6 select_reduce_fusion.idx
  1.3 0.0 copy-done
  1.3 232.1 %attend_all.1 = bf16[32,16,2048]{2,1,0:T(8,128)(2,1)} custom-call(s32[64]{0:T(128)} %select_reduce_fusion.idx, s32[32]{0:T(128)} %copy-done, bf16[32,16,2048]{2,1,0:T(8,128)(2,1)} %bitcast.18, bf16[4,128,256]{2,1,0:T(8,128)(2,1)} %bitcast.19, bf16[4,128,256]{2,1,0:T(8,128)(2,1)} %bitcast.20, bf16[512,1024]{1,0:T(8,128)(2,1)} %pk.1, bf16[512,1024]{1,0:T(8,128)(2,1)} %pv.1), custom_call_target="tpu_custom_call" | custom-call | tf_op jit(solution)/shard_map/attend_all/pallas_call | solution.py:343
  233.4 3.2 %copy.8 = bf16[512,2048]{1,0:T(8,128)(2,1)} copy(bf16[512,2048]{1,0:T(8,128)(2,1)} %bitcast.17) | data formatting | bytes 4194304
Async XLA Ops:
  0.7 0.6 copy-start

commit v2 on v1

--- a/solution.py
+++ b/solution.py
@@ -43,15 +43,21 @@
 
 
 def kernel(
-    idx, pos, q, ck, cv, pk, pv, out,
-    cache, qs, fs, nq, relay_q, fq, no, fo, relay_o, ret, own, own_lse,
-    send_sem, recv_sem, local_sem,
+    table, q_in, ck_in, cv_in, pk, pv, out,
+    q, ck, cv, cache, qs, fs, nq, relay_q, fq, no, fo, relay_o, ret0, ret1, own, own_lse,
+    send_sem, recv_sem, local_sem, load_sem,
 ):
     dp, x = lax.axis_index("dp"), lax.axis_index("mp")
     z, lane = dp // PLANE, dp % PLANE
     xs = lax.axis_size("mp")
     share = pk.shape[0]
     comps = q.shape[0]
+    loads = [
+        pltpu.make_async_copy(src, dst, load_sem.at[n])
+        for n, (src, dst) in enumerate(((q_in, q), (ck_in, ck), (cv_in, cv)))
+    ]
+    for load in loads:
+        load.start()
 
     def to_x(e):
         return (dp, (x + e) % xs)
@@ -70,6 +76,14 @@
     )
     for friend in friends:
         pl.semaphore_signal(barrier, 1, device_id=friend, device_id_type=MESH)
+
+    def pack(dst, at, d, rr):
+        dst[at] = q[table[rr * PLANE + d]]
+
+    loads[0].wait()
+    for rr in range(3):
+        for d in range(PLANE):
+            pack(fs, (rr, d), d, 5 + rr)
     pl.semaphore_wait(barrier, len(friends))
 
     count = [0]
@@ -108,30 +122,32 @@
         for copy in copies[1:]:
             copy.wait_recv()
 
-    def spread(h, w, places):
-        return {j: remote(cache.at[0, h, w], cache.at[j, h, w], to_z(k)) for j, k in places}
-
-    EDGE, NEXT = ((3, -2), (4, 2)), ((1, -1), (2, 1))
-
+    def spread(h, w):
+        return [remote(cache.at[0, h, w], cache.at[j, h, w], to_z(k)) for j, k in ((1, -1), (2, 1))]
+
+    def relay(h, w, copies):
+        for copy in copies:
+            copy.wait_recv()
+        return [remote(cache.at[j, h, w], cache.at[j + 2, h, w], to_z(k)) for j, k in ((1, -1), (2, 1))]
+
+    half = PLANE // 2
+    far_z = [
+        remote(fs.at[0], relay_q.at[:, 0], to_z(1)),
+        remote(fs.at[1], relay_q.at[:, 1], to_z(-1)),
+        remote(fs.at[2, pl.ds(0, half)], relay_q.at[pl.ds(0, half), 2], to_z(2)),
+        remote(fs.at[2, pl.ds(half, half)], relay_q.at[pl.ds(half, half), 2], to_z(-2)),
+    ]
     parts0 = exchange(0)
-
-    def pack(d, first, last, dst):
-        for rr in range(first, last):
-            dst[rr - first] = q[idx[d * RING + rr]]
-
-    pack(0, 5, 8, relay_q.at[0])
-    for d in range(1, PLANE):
-        pack(d, 5, 8, fs.at[d])
-    far_y = [remote(fs.at[d], relay_q.at[d], to_lane(d)) for d in range(1, PLANE)]
-    pack(0, 0, 5, nq.at[0])
-    for d in range(1, PLANE):
-        pack(d, 0, 5, qs.at[d])
+    for rr in range(5):
+        pack(nq, (0, rr), 0, rr)
+        for d in range(1, PLANE):
+            pack(qs, (d, rr), d, rr)
     near_y = [remote(qs.at[d], nq.at[d], to_lane(d)) for d in range(1, PLANE)]
 
-    spread0 = []
+    next0 = []
     for w in range(2):
         arrive(parts0[w])
-        spread0.append({**spread(0, w, EDGE), **spread(0, w, NEXT)})
+        next0.append(spread(0, w))
     parts1 = exchange(1)
 
     block = HD // LEN
@@ -168,17 +184,18 @@
                 own_lse[b * block + c, h] = by_group(lse[c * HD : (c + 1) * HD])
         return carry
 
+    for load in loads[1:]:
+        load.wait()
     lax.fori_loop(0, comps // block, own_block, 0)
 
-    for copy in far_y:
+    next1 = []
+    for w in range(2):
+        arrive(parts1[w])
+        next1.append(spread(1, w))
+    for copy in far_z:
         copy.wait_recv()
-    half = PLANE // 2
-    far_q = [
-        remote(relay_q.at[:, 0], fq.at[pl.ds(0, 8)], to_z(1)),
-        remote(relay_q.at[:, 1], fq.at[pl.ds(12, 8)], to_z(-1)),
-        remote(relay_q.at[pl.ds(0, half), 2], fq.at[pl.ds(8, half)], to_z(2)),
-        remote(relay_q.at[pl.ds(half, half), 2], fq.at[pl.ds(20, half)], to_z(-2)),
-    ]
+    far_y = [remote(relay_q.at[d], fq.at[d], to_lane(d)) for d in range(1, PLANE)]
+    fq[0] = relay_q[0]
 
     def attend(queries, j, h):
         pieces = []
@@ -210,6 +227,8 @@
         for g, piece in enumerate(pieces):
             dst[i + (slice(None), slice(g * HD, (g + 1) * HD))] = piece
 
+    ret = (ret0, ret1)
+
     def head(h):
         return slice(h * SLOT, (h + 1) * SLOT)
 
@@ -223,101 +242,99 @@
 
         lax.fori_loop(0, (last - first) * (PLANE // 2), step, 0)
 
-    def far(h):
+    def far(h, k):
         def step(n, carry):
-            two = attend([fq[2 * n, :, head(h)], fq[2 * n + 1, :, head(h)]], 3 + n // 6, h)
-            for k in range(2):
-                put(fo, (h, 2 * n + k), two[k])
+            d = 2 * n
+            j = 3 + n // (half // 2) if k == 2 else 3 + k
+            two = attend([fq[d, k, :, head(h)], fq[d + 1, k, :, head(h)]], j, h)
+            for i in range(2):
+                put(fo, (h, k, d + i), two[i])
             return carry
 
-        lax.fori_loop(0, 12, step, 0)
+        lax.fori_loop(0, half, step, 0)
+        relay_o[h, k, 0] = fo[h, k, 0]
+        return [remote(fo.at[h, k, d], relay_o.at[h, k, d], to_lane(-d)) for d in range(1, PLANE)]
 
     returned = []
+
+    def pass_far(h, k, copies):
+        for copy in copies:
+            copy.wait_recv()
+        if k < 2:
+            returned.append(remote(relay_o.at[h, k], ret[h].at[5 + k], to_z(2 * k - 1)))
+        else:
+            for n in range(2):
+                span = pl.ds(n * half, half)
+                returned.append(remote(relay_o.at[h, 2, span], ret[h].at[7, span], to_z(4 * n - 2)))
 
     def give_near(h, first, last):
         span = pl.ds(first, last - first)
         for d in range(1, PLANE):
-            returned.append(remote(no.at[h, d, span], ret.at[h, pl.ds(d * RING + first, last - first)], to_lane(-d)))
-        ret[h, first:last] = no[h, 0, first:last]
-
-    def give_far(h):
-        return [
-            remote(fo.at[h, pl.ds(0, 8)], relay_o.at[h, 0], to_z(-1)),
-            remote(fo.at[h, pl.ds(12, 8)], relay_o.at[h, 1], to_z(1)),
-            remote(fo.at[h, pl.ds(8, half)], relay_o.at[h, 2, pl.ds(0, half)], to_z(-2)),
-            remote(fo.at[h, pl.ds(20, half)], relay_o.at[h, 2, pl.ds(half, half)], to_z(2)),
-        ]
-
-    def pass_far(h, copies):
-        for rr in range(3):
-            for copy in (copies[rr : rr + 1] if rr < 2 else copies[2:]):
-                copy.wait_recv()
-            for d in range(1, PLANE):
-                returned.append(remote(relay_o.at[h, rr, d], ret.at[h, d * RING + 5 + rr], to_lane(-d)))
-            ret[h, 5 + rr] = relay_o[h, rr, 0]
-
-    for w in range(2):
-        arrive(parts1[w])
+            returned.append(remote(no.at[h, d, span], ret[h].at[span, d], to_lane(-d)))
+        for j in range(first, last):
+            ret[h][j, 0] = no[h, 0, j]
+
     for copy in near_y:
         copy.wait_recv()
     near(0, 0, 1)
+    edge0 = [relay(0, w, next0[w]) for w in range(2)]
     near(1, 0, 1)
-
-    for copies in spread0:
-        for copy in copies.values():
-            copy.wait_send()
-    edge1 = [spread(1, w, EDGE) for w in range(2)]
-    for copies in spread0:
-        for copy in copies.values():
-            copy.wait_recv()
-    near(0, 1, 5)
-    give_near(0, 0, 5)
-    for copy in far_q:
-        copy.wait_recv()
-    far(0)
-    back0 = give_far(0)
-    next1 = [spread(1, w, NEXT) for w in range(2)]
-
-    for copies in edge1:
-        for copy in copies.values():
-            copy.wait_recv()
-    far(1)
-    back1 = give_far(1)
-    pass_far(0, back0)
-    near(1, 3, 5)
-    give_near(1, 3, 5)
-    for copies in next1:
-        for copy in copies.values():
-            copy.wait_recv()
+    near(0, 1, 3)
+    give_near(0, 0, 3)
+    edge1 = [relay(1, w, next1[w]) for w in range(2)]
     near(1, 1, 3)
     give_near(1, 0, 3)
-    pass_far(1, back1)
-    for copy in returned:
+    for copy in far_y:
         copy.wait_recv()
-
-    def blend(c, carry):
-        for h in range(HEADS):
-            slot = ret[h, pos[c]]
-            tail = slot[:, SLOT:].astype(jnp.float32)
-            far_lse = tail[:, :GROUP] + tail[:, GROUP : 2 * GROUP] + tail[:, 2 * GROUP : 3 * GROUP]
-            near_lse = own_lse[c, h][:, :GROUP]
-            ceiling = jnp.maximum(far_lse, near_lse)
-            a, b = jnp.exp(far_lse - ceiling), jnp.exp(near_lse - ceiling)
-            inverse = 1.0 / (a + b)
-            a, b = a * inverse, b * inverse
-            for g in range(GROUP):
-                part = slice(h * SLOT + g * HD, h * SLOT + (g + 1) * HD)
-                out[c, :, part] = (
-                    slot[:, g * HD : (g + 1) * HD].astype(jnp.float32) * a[:, g : g + 1]
-                    + own[c, :, part] * b[:, g : g + 1]
-                ).astype(jnp.bfloat16)
-        return carry
-
-    lax.fori_loop(0, comps, blend, 0)
-    already = {id(copy) for copies in spread0 for copy in copies.values()}
+    for copies in edge0:
+        for copy in copies:
+            copy.wait_recv()
+    back = {k: far(0, k) for k in (2, 0, 1)}
+    near(0, 3, 5)
+    give_near(0, 3, 5)
+    for k in (2, 0, 1):
+        pass_far(0, k, back[k])
+    first = len(returned)
+    for copies in edge1:
+        for copy in copies:
+            copy.wait_recv()
+    back = {2: far(1, 2), 0: far(1, 0)}
+    pass_far(1, 2, back[2])
+    back[1] = far(1, 1)
+    pass_far(1, 0, back[0])
+    near(1, 3, 4)
+    give_near(1, 3, 4)
+    pass_far(1, 1, back[1])
+    near(1, 4, 5)
+    give_near(1, 4, 5)
+
+    def blend(h):
+        def step(n, carry):
+            for c in [n * 4 + i for i in range(4)]:
+                slot = ret[h][table[PLANE * RING + c], table[PLANE * RING + comps + c]]
+                tail = slot[:, SLOT:].astype(jnp.float32)
+                far_lse = tail[:, :GROUP] + tail[:, GROUP : 2 * GROUP] + tail[:, 2 * GROUP : 3 * GROUP]
+                near_lse = own_lse[c, h][:, :GROUP]
+                ceiling = jnp.maximum(far_lse, near_lse)
+                a, b = jnp.exp(far_lse - ceiling), jnp.exp(near_lse - ceiling)
+                a = a / (a + b)
+                for g in range(GROUP):
+                    part = slice(h * SLOT + g * HD, h * SLOT + (g + 1) * HD)
+                    mine = own[c, :, part]
+                    theirs = slot[:, g * HD : (g + 1) * HD].astype(jnp.float32)
+                    out[c, :, part] = (mine + (theirs - mine) * a[:, g : g + 1]).astype(jnp.bfloat16)
+            return carry
+
+        lax.fori_loop(0, comps // 4, step, 0)
+
+    for copy in returned[:first]:
+        copy.wait_recv()
+    blend(0)
+    for copy in returned[first:]:
+        copy.wait_recv()
+    blend(1)
     for copy in sent:
-        if id(copy) not in already:
-            copy.wait_send()
+        copy.wait_send()
 
 
 def body(queries, comp_keys, comp_values, prefix_keys, prefix_values, prompt_of):
@@ -329,11 +346,15 @@
     place = jnp.zeros_like(distance)
     for n, r in enumerate(ORDER):
         place = jnp.where(distance == r, n, place)
-    pos = offset * RING + place
-    slots = jnp.arange(PLANE * RING)
-    idx = jnp.sum(
-        jnp.where(pos[None, :] == slots[:, None], jnp.arange(comps)[None, :], 0), axis=1
-    ).astype(jnp.int32)
+    pos = place * PLANE + offset
+    t, c = jnp.arange(PLANE * RING + 2 * comps)[:, None], jnp.arange(comps)[None, :]
+    entry = jnp.where(
+        t < PLANE * RING,
+        jnp.where(pos[None, :] == t, c, 0),
+        jnp.where(c == t - PLANE * RING, place[None, :], 0)
+        + jnp.where(c == t - PLANE * RING - comps, offset[None, :], 0),
+    )
+    table = jnp.sum(entry, axis=1).astype(jnp.int32)
     keys = prefix_keys.shape[0] * lax.axis_size("mp")
     bf16 = jnp.bfloat16
     blocks = comp_keys.shape[0] // HD
@@ -343,32 +364,36 @@
     out = pl.pallas_call(
         kernel,
         out_shape=jax.ShapeDtypeStruct((comps, LEN, queries.shape[1]), bf16),
-        in_specs=[smem, smem, vmem, vmem, vmem, hbm, hbm],
+        in_specs=[smem, hbm, hbm, hbm, hbm, hbm],
         out_specs=vmem,
         scratch_shapes=[
+            pltpu.VMEM((comps, LEN, HEADS * SLOT), bf16),
+            pltpu.VMEM((blocks, HD, HEADS * HD), bf16),
+            pltpu.VMEM((blocks, HD, HEADS * HD), bf16),
             pltpu.VMEM((5, HEADS, 2, keys, HD), bf16),
             pltpu.VMEM((PLANE, 5, LEN, HEADS * SLOT), bf16),
-            pltpu.VMEM((PLANE, 3, LEN, HEADS * SLOT), bf16),
+            pltpu.VMEM((3, PLANE, LEN, HEADS * SLOT), bf16),
             pltpu.VMEM((PLANE, 5, LEN, HEADS * SLOT), bf16),
             pltpu.VMEM((PLANE, 3, LEN, HEADS * SLOT), bf16),
-            pltpu.VMEM((24, LEN, HEADS * SLOT), bf16),
+            pltpu.VMEM((PLANE, 3, LEN, HEADS * SLOT), bf16),
             pltpu.VMEM((HEADS, PLANE, 5, LEN, WIDE), bf16),
-            pltpu.VMEM((HEADS, 24, LEN, WIDE), bf16),
             pltpu.VMEM((HEADS, 3, PLANE, LEN, WIDE), bf16),
-            pltpu.VMEM((HEADS, PLANE * RING, LEN, WIDE), bf16),
+            pltpu.VMEM((HEADS, 3, PLANE, LEN, WIDE), bf16),
+            pltpu.VMEM((RING, PLANE, LEN, WIDE), bf16),
+            pltpu.VMEM((RING, PLANE, LEN, WIDE), bf16),
             pltpu.VMEM((comps, LEN, HEADS * SLOT), jnp.float32),
             pltpu.VMEM((comps, HEADS, LEN, HD), jnp.float32),
             pltpu.SemaphoreType.DMA((copies,)),
             pltpu.SemaphoreType.DMA((copies,)),
             pltpu.SemaphoreType.DMA((4,)),
+            pltpu.SemaphoreType.DMA((3,)),
         ],
         compiler_params=pltpu.CompilerParams(
             collective_id=0, has_side_effects=True, vmem_limit_bytes=60 * 1024 * 1024
         ),
         name="attend_all",
     )(
-        idx,
-        pos,
+        table,
         queries.reshape(comps, LEN, -1),
         comp_keys.reshape(blocks, HD, -1),
         comp_values.reshape(blocks, HD, -1),

time: 237 us -> 164 us (0.69)
  Pallas kernels: 232 us -> 159 us
    pallas_call x1, Pallas kernels: 232 us -> 159 us  [body(): pl.pallas_call(kernel, out_shape=jax.ShapeDtypeStruct((comps, LEN, querie...]
where the time goes in v2:
time: 164 us
  Pallas kernels  159 us (97%)
  local copies, waits for them, and re-layouts  3.16 us (2%)
    pallas_call x1, Pallas kernels, body(): pl.pallas_call(kernel, out_shape=jax.ShapeDtypeStruct((comps, LEN, querie...  159 us

profile of v2, /device:TPU:1, one launch (start us, length us, event | category | flops | bytes accessed | tf_op | source)
XLA Modules:
  0.0 163.7 jit_solution(6448757197303335665)
XLA Ops:
  0.0 0.7 multiply_add_fusion
  0.7 0.6 select_reduce_fusion.table
  1.3 159.2 %attend_all.1 = bf16[32,16,2048]{2,1,0:T(8,128)(2,1)} custom-call(s32[128]{0:T(128)} %select_reduce_fusion.table, bf16[32,16,2048]{2,1,0:T(8,128)(2,1)} %bitcast.24, bf16[4,128,256]{2,1,0:T(8,128)(2,1)} %bitcast.25, bf16[4,128,256]{2,1,0:T(8,128)(2,1)} %bitcast.26, bf16[512,1024]{1,0:T(8,128)(2,1)} %pk.1, bf16[512,1024]{1,0:T(8,128)(2,1)} %pv.1), custom_call_target="tpu_custom_call" | custom-call | tf_op jit(solution)/shard_map/attend_all/pallas_call | solution.py:364
  160.5 3.2 %copy.8 = bf16[512,2048]{1,0:T(8,128)(2,1)} copy(bf16[512,2048]{1,0:T(8,128)(2,1)} %bitcast.23) | data formatting | bytes 4194304
  (2 shorter events, 0.0 us)

commit v3 on v2

v3 whole, which is shorter than its diff:
```python
import functools
import math

import jax
import jax.numpy as jnp
from jax import lax
from jax.experimental import pallas as pl
from jax.experimental.pallas import tpu as pltpu
from jax.sharding import PartitionSpec as P

MESH = pl.DeviceIdType.MESH
HD = 128
LEN = 16
GROUP = 8
HEADS = 2
PLANE = 8
RING = 8
SLOT = GROUP * HD
WIDE = SLOT + HD
SCALE = 1.0 / math.sqrt(HD)
LOG2E = math.log2(math.e)
ORDER = (0, 1, 7, 2, 6, 3, 5, 4)


def split3(x):
    hi = x.astype(jnp.bfloat16)
    rest = x - hi.astype(jnp.float32)
    mid = rest.astype(jnp.bfloat16)
    low = (rest - mid.astype(jnp.float32)).astype(jnp.bfloat16)
    return hi, mid, low


def by_group(column):
    lane = lax.broadcasted_iota(jnp.int32, (LEN, HD), 1)
    out = jnp.zeros((LEN, HD), jnp.float32)
    for g in range(GROUP):
        out = jnp.where(lane == g, column[g * LEN : (g + 1) * LEN], out)
    return out


def rows_of(slot):
    return [slot[:, g * HD : (g + 1) * HD] for g in range(GROUP)]


def kernel(
    table, prompt, q_in, ck_in, cv_in, pk, pv, out,
    q, ck, cv, cache, qs, fs, nq, relay_q, fq, no, fo, relay_o, ret0, ret1, own, own_lse,
    mixed, send_sem, recv_sem, local_sem, load_sem, out_sem,
):
    dp, x = lax.axis_index("dp"), lax.axis_index("mp")
    z, lane = dp // PLANE, dp % PLANE
    xs = lax.axis_size("mp")
    share = pk.shape[0]
    comps = q.shape[0]
    loads = [
        pltpu.make_async_copy(src, dst, load_sem.at[n])
        for n, (src, dst) in enumerate(((q_in, q), (ck_in, ck), (cv_in, cv)))
    ]
    for load in loads:
        load.start()

    def to_x(e):
        return (dp, (x + e) % xs)

    def to_z(k):
        return (((z + k + RING) % RING) * PLANE + lane, x)

    def to_lane(d):
        return (z * PLANE + (lane + d + PLANE) % PLANE, x)

    barrier = pltpu.get_barrier_semaphore()
    friends = (
        [to_x(e) for e in range(1, xs)]
        + [to_z(k) for k in (1, -1, 2, -2)]
        + [to_lane(d) for d in range(1, PLANE)]
    )
    for friend in friends:
        pl.semaphore_signal(barrier, 1, device_id=friend, device_id_type=MESH)

    def pack(dst, at, d, rr):
        dst[at] = q[table[rr * PLANE + d]]

    loads[0].wait()
    for rr in range(3):
        for d in range(PLANE):
            pack(fs, (rr, d), d, 5 + rr)
    pl.semaphore_wait(barrier, len(friends))

    count = [0]
    sent = []

    def remote(parts, src, dst):
        n = count[0]
        count[0] += 1
        for part_src, part_dst, device in parts:
            pltpu.make_async_remote_copy(
                src_ref=part_src, dst_ref=part_dst, send_sem=send_sem.at[n], recv_sem=recv_sem.at[n],
                device_id=device, device_id_type=MESH,
            ).start()
        whole = pltpu.make_async_remote_copy(
            src_ref=src, dst_ref=dst, send_sem=send_sem.at[n], recv_sem=recv_sem.at[n],
            device_id=parts[0][2], device_id_type=MESH,
        )
        sent.append(whole)
        return whole

    def columns(e, h):
        return pl.ds(pl.multiple_of(((x + e) % xs) * (HEADS * HD) + h * HD, HD), HD)

    def exchange(h):
        copies = []
        for w, whole in enumerate((pk, pv)):
            mine = pltpu.make_async_copy(
                whole.at[:, columns(0, h)], cache.at[0, h, w, pl.ds(0, share)],
                local_sem.at[h * 2 + w],
            )
            mine.start()
            others = cache.at[0, h, w, pl.ds(share, (xs - 1) * share)]
            copies.append((mine, remote(
                [
                    (whole.at[:, columns(e, h)], cache.at[0, h, w, pl.ds(e * share, share)], to_x(e))
                    for e in range(1, xs)
                ],
                others,
                others,
            )))
        return copies

    def arrive(copies):
        copies[0].wait()
        copies[1].wait_recv()

    def spread(h, w):
        both = cache.at[pl.ds(1, 2), h, w]
        return remote(
            [(cache.at[0, h, w], cache.at[j, h, w], to_z(k)) for j, k in ((1, -1), (2, 1))], both, both
        )

    def relay(h, w, copy):
        copy.wait_recv()
        return remote(
            [(cache.at[j, h, w], cache.at[j + 2, h, w], to_z(k)) for j, k in ((1, -1), (2, 1))],
            cache.at[pl.ds(1, 2), h, w],
            cache.at[pl.ds(3, 2), h, w],
        )

    half = PLANE // 2
    def along(k, src, dst, sign):
        if k < 2:
            return remote([(src, dst, to_z(sign * (1 - 2 * k)))], src, dst)
        spans = [pl.ds(n * half, half) for n in range(2)]
        return remote(
            [(src.at[span], dst.at[span], to_z(sign * (2 - 4 * n))) for n, span in enumerate(spans)], src, dst
        )

    far_z = [along(k, fs.at[k], relay_q.at[:, k], 1) for k in range(3)]
    parts0 = exchange(0)
    for rr in range(5):
        pack(nq, (0, rr), 0, rr)
        for d in range(1, PLANE):
            pack(qs, (d, rr), d, rr)
    lanes = pl.ds(1, PLANE - 1)
    near_y = remote(
        [(qs.at[d], nq.at[d], to_lane(d)) for d in range(1, PLANE)], qs.at[lanes], nq.at[lanes]
    )

    next0 = []
    for w in range(2):
        arrive(parts0[w])
        next0.append(spread(0, w))
    parts1 = exchange(1)

    block = HD // LEN
    rows = block * HD
    r_at = lax.broadcasted_iota(jnp.int32, (rows, HD), 0)
    c_at = lax.broadcasted_iota(jnp.int32, (rows, HD), 1)
    allowed = (r_at // HD == c_at // LEN) & (r_at % LEN >= c_at % LEN)

    def own_block(b, carry):
        keys, values = ck[b], cv[b]
        for h in range(HEADS):
            pieces = []
            for c in range(block):
                pieces += rows_of(q[b * block + c, :, h * SLOT : (h + 1) * SLOT])
            part = slice(h * HD, (h + 1) * HD)
            s = lax.dot_general(
                jnp.concatenate(pieces, axis=0), keys[:, part], (((1,), (1,)), ((), ())),
                preferred_element_type=jnp.float32,
            ) * SCALE
            s = jnp.where(allowed, s, -1e30)
            top = jnp.max(s, axis=1, keepdims=True)
            w = jnp.exp(s - top)
            total = jnp.sum(w, axis=1, keepdims=True)
            mixed = jnp.dot(
                w.astype(jnp.bfloat16), values[:, part], preferred_element_type=jnp.float32
            ) / total
            lse = top + jnp.log(total)
            for c in range(block):
                for g in range(GROUP):
                    at = c * HD + g * LEN
                    own[b * block + c, :, h * SLOT + g * HD : h * SLOT + (g + 1) * HD] = (
                        mixed[at : at + LEN]
                    )
                own_lse[b * block + c, h] = by_group(lse[c * HD : (c + 1) * HD])
        return carry

    for load in loads[1:]:
        load.wait()
    lax.fori_loop(0, comps // block, own_block, 0)

    next1 = []
    for w in range(2):
        arrive(parts1[w])
        next1.append(spread(1, w))
    for copy in far_z:
        copy.wait_recv()
    far_y = remote(
        [(relay_q.at[d], fq.at[d], to_lane(d)) for d in range(1, PLANE)], relay_q.at[lanes], fq.at[lanes]
    )
    fq[0] = relay_q[0]

    def attend(queries, j, h):
        scores, results = [], []
        for slot in queries:
            scores.append(lax.dot_general(
                jnp.concatenate(rows_of(slot[0]) + rows_of(slot[1]), axis=0), cache[j, h, 0],
                (((1,), (1,)), ((), ())), preferred_element_type=jnp.float32,
            ))
        for s in scores:
            top = jnp.max(s, axis=1, keepdims=True)
            w = jnp.exp2((s - top) * (SCALE * LOG2E))
            total = jnp.sum(w, axis=1, keepdims=True)
            mixed = jnp.dot(w.astype(jnp.bfloat16), cache[j, h, 1], preferred_element_type=jnp.float32)
            mixed = (mixed / total).astype(jnp.bfloat16)
            lse = top * SCALE + jnp.log(total)
            for at in (0, HD):
                hi, mid, low = split3(by_group(lse[at : at + HD]))
                tail = jnp.concatenate(
                    [hi[:, :GROUP], mid[:, :GROUP], low[:, :GROUP], hi[:, 3 * GROUP :]], axis=1
                )
                results.append(
                    [mixed[at + g * LEN : at + (g + 1) * LEN] for g in range(GROUP)] + [tail]
                )
        return results

    def put(dst, i, pieces):
        for g, piece in enumerate(pieces):
            dst[i + (slice(None), slice(g * HD, (g + 1) * HD))] = piece

    ret = (ret0, ret1)

    def head(h):
        return slice(h * SLOT, (h + 1) * SLOT)

    def near(h, first, last):
        def step(n, carry):
            j, d = first + n // 2, half * (n % 2)
            four = attend([[nq[d + i + k, j, :, head(h)] for k in range(2)] for i in (0, 2)], j, h)
            for k in range(4):
                put(no, (h, d + k, j), four[k])
            return carry

        lax.fori_loop(0, (last - first) * 2, step, 0)

    def far(h, k):
        def step(n, carry):
            d = half * n
            j = 3 + n if k == 2 else 3 + k
            four = attend([[fq[d + i + m, k, :, head(h)] for m in range(2)] for i in (0, 2)], j, h)
            for i in range(4):
                put(fo, (h, k, d + i), four[i])
            return carry

        lax.fori_loop(0, 2, step, 0)
        relay_o[h, k, 0] = fo[h, k, 0]
        return remote(
            [(fo.at[h, k, d], relay_o.at[h, k, d], to_lane(-d)) for d in range(1, PLANE)],
            fo.at[h, k, lanes],
            relay_o.at[h, k, lanes],
        )

    returned = []

    def pass_far(h, k, copy):
        copy.wait_recv()
        returned.append(along(k, relay_o.at[h, k], ret[h].at[5 + k], -1))

    def give_near(h, first, last):
        span = pl.ds(first, last - first)
        returned.append(remote(
            [(no.at[h, d, span], ret[h].at[span, d], to_lane(-d)) for d in range(1, PLANE)],
            no.at[h, lanes, span],
            ret[h].at[span, lanes],
        ))
        for j in range(first, last):
            ret[h][j, 0] = no[h, 0, j]

    near_y.wait_recv()
    near(0, 0, 1)
    edge0 = [relay(0, w, next0[w]) for w in range(2)]
    near(1, 0, 1)
    near(0, 1, 3)
    give_near(0, 0, 3)
    edge1 = [relay(1, w, next1[w]) for w in range(2)]
    near(1, 1, 3)
    give_near(1, 0, 3)
    far_y.wait_recv()
    for copy in edge0:
        copy.wait_recv()
    back = {k: far(0, k) for k in (2, 0, 1)}
    near(0, 3, 5)
    give_near(0, 3, 5)
    for k in (2, 0, 1):
        pass_far(0, k, back[k])
    first = len(returned)
    for copy in edge1:
        copy.wait_recv()
    back = {2: far(1, 2), 0: far(1, 0)}
    pass_far(1, 2, back[2])
    back[1] = far(1, 1)
    pass_far(1, 0, back[0])
    near(1, 3, 4)
    give_near(1, 3, 4)
    pass_far(1, 1, back[1])
    near(1, 4, 5)
    give_near(1, 4, 5)

    def write(h, n):
        span = pl.ds(n * 4, 4)
        return pltpu.make_async_copy(
            mixed.at[h, span], out.at[span, :, pl.ds(h * SLOT, SLOT)], out_sem.at[h, n]
        )

    def blend(h):
        def step(n, carry):
            for i in range(4):
                c = n * 4 + i
                distance = (prompt[c] // PLANE - z + RING) % RING
                place = jnp.where(
                    distance < 3,
                    distance + distance // 2,
                    jnp.where(distance < 6, 5 + (distance - 3) * 2 - (distance - 3) // 2 * 3, 16 - 2 * distance),
                )
                slot = ret[h][place, (prompt[c] - lane + PLANE) % PLANE]
                tail = slot[:, SLOT:].astype(jnp.float32)
                far_lse = tail[:, :GROUP] + tail[:, GROUP : 2 * GROUP] + tail[:, 2 * GROUP : 3 * GROUP]
                near_lse = own_lse[c, h][:, :GROUP]
                ceiling = jnp.maximum(far_lse, near_lse)
                a, b = jnp.exp(far_lse - ceiling), jnp.exp(near_lse - ceiling)
                a = a / (a + b)
                for g in range(GROUP):
                    part = slice(g * HD, (g + 1) * HD)
                    mine = own[c, :, h * SLOT + g * HD : h * SLOT + (g + 1) * HD]
                    theirs = slot[:, part].astype(jnp.float32)
                    mixed[h, c, :, part] = (mine + (theirs - mine) * a[:, g : g + 1]).astype(jnp.bfloat16)
            write(h, n).start()
            return carry

        lax.fori_loop(0, comps // 4, step, 0)

    for copy in returned[:first]:
        copy.wait_recv()
    blend(0)
    for copy in returned[first:]:
        copy.wait_recv()
    blend(1)
    for copy in sent:
        copy.wait_send()
    for h in range(HEADS):
        for n in range(comps // 4):
            write(h, n).wait()


def hand_over(src, dst, held, sems):
    parts, rows = held.shape[:2]
    spans = [pl.ds(n * rows, rows) for n in range(parts)]
    ins = [pltpu.make_async_copy(src.at[span], held.at[n], sems.at[0, n]) for n, span in enumerate(spans)]
    outs = [pltpu.make_async_copy(held.at[n], dst.at[span], sems.at[1, n]) for n, span in enumerate(spans)]
    for copy in ins:
        copy.start()
    for n in range(parts):
        ins[n].wait()
        outs[n].start()
    for copy in outs:
        copy.wait()


def body(queries, comp_keys, comp_values, prefix_keys, prefix_values, prompt_of):
    comps = prompt_of.shape[0]
    dp = lax.axis_index("dp")
    prompt = prompt_of[:, 0]
    slot = jnp.arange(PLANE * RING)
    place = slot // PLANE
    distance = jnp.zeros_like(place)
    for n, r in enumerate(ORDER):
        distance = jnp.where(place == n, r, distance)
    wanted = (dp // PLANE + distance) % RING * PLANE + (dp + slot) % PLANE
    named = prompt[None, :] == wanted[:, None]
    table = jnp.sum(jnp.where(named, jnp.arange(comps)[None, :], 0), axis=1).astype(jnp.int32)
    keys = prefix_keys.shape[0] * lax.axis_size("mp")
    bf16 = jnp.bfloat16
    blocks = comp_keys.shape[0] // HD
    vmem, smem = pl.BlockSpec(memory_space=pltpu.VMEM), pl.BlockSpec(memory_space=pltpu.SMEM)
    hbm = pl.BlockSpec(memory_space=pl.ANY)
    copies = 34
    out = pl.pallas_call(
        kernel,
        out_shape=jax.ShapeDtypeStruct((comps, LEN, queries.shape[1]), bf16),
        in_specs=[smem, smem, hbm, hbm, hbm, hbm, hbm],
        out_specs=hbm,
        scratch_shapes=[
            pltpu.VMEM((comps, LEN, HEADS * SLOT), bf16),
            pltpu.VMEM((blocks, HD, HEADS * HD), bf16),
            pltpu.VMEM((blocks, HD, HEADS * HD), bf16),
            pltpu.VMEM((5, HEADS, 2, keys, HD), bf16),
            pltpu.VMEM((PLANE, 5, LEN, HEADS * SLOT), bf16),
            pltpu.VMEM((3, PLANE, LEN, HEADS * SLOT), bf16),
            pltpu.VMEM((PLANE, 5, LEN, HEADS * SLOT), bf16),
            pltpu.VMEM((PLANE, 3, LEN, HEADS * SLOT), bf16),
            pltpu.VMEM((PLANE, 3, LEN, HEADS * SLOT), bf16),
            pltpu.VMEM((HEADS, PLANE, 5, LEN, WIDE), bf16),
            pltpu.VMEM((HEADS, 3, PLANE, LEN, WIDE), bf16),
            pltpu.VMEM((HEADS, 3, PLANE, LEN, WIDE), bf16),
            pltpu.VMEM((RING, PLANE, LEN, WIDE), bf16),
            pltpu.VMEM((RING, PLANE, LEN, WIDE), bf16),
            pltpu.VMEM((comps, LEN, HEADS * SLOT), jnp.float32),
            pltpu.VMEM((comps, HEADS, LEN, HD), jnp.float32),
            pltpu.VMEM((HEADS, comps, LEN, SLOT), bf16),
            pltpu.SemaphoreType.DMA((copies,)),
            pltpu.SemaphoreType.DMA((copies,)),
            pltpu.SemaphoreType.DMA((4,)),
            pltpu.SemaphoreType.DMA((3,)),
            pltpu.SemaphoreType.DMA((HEADS, comps // 4)),
        ],
        compiler_params=pltpu.CompilerParams(
            collective_id=0, has_side_effects=True, vmem_limit_bytes=60 * 1024 * 1024
        ),
        name="attend_all",
    )(
        table,
        prompt,
        queries.reshape(comps, LEN, -1),
        comp_keys.reshape(blocks, HD, -1),
        comp_values.reshape(blocks, HD, -1),
        prefix_keys,
        prefix_values,
    )
    return pl.pallas_call(
        hand_over,
        out_shape=jax.ShapeDtypeStruct(queries.shape, bf16),
        in_specs=[hbm],
        out_specs=hbm,
        scratch_shapes=[
            pltpu.VMEM((8, queries.shape[0] // 8, queries.shape[1]), bf16),
            pltpu.SemaphoreType.DMA((2, 8)),
        ],
        name="hand_over",
    )(out.reshape(queries.shape))


def solution(mesh):
    placed = (
        P("dp", "mp"),
        P("dp", "mp"),
        P("dp", "mp"),
        P(("dp", "mp"), None),
        P(("dp", "mp"), None),
        P("dp", None),
    )
    return jax.shard_map(body, mesh=mesh, in_specs=placed, out_specs=P("dp", "mp"), check_vma=False)
```

time: 164 us -> 160 us (0.976)
  local copies, waits for them, and re-layouts: 3.16 us -> 0 us
    pallas_call x1, Pallas kernels: 159 us -> 156 us  [body(): pl.pallas_call(kernel, out_shape=jax.ShapeDtypeStruct((comps, LEN, querie...]
    unnamed x1 -> x0, local copies, waits for them, and re-layouts: 3.16 us -> none
    pallas_call x0 -> x1, Pallas kernels: none -> 2.4 us  [body(): pl.pallas_call(hand_over, out_shape=jax.ShapeDtypeStruct(queries.shape, b...]
where the time goes in v3:
time: 160 us
  Pallas kernels  158 us (99%)
    pallas_call x1, Pallas kernels, body(): pl.pallas_call(kernel, out_shape=jax.ShapeDtypeStruct((comps, LEN, querie...  156 us

profile of v3, /device:TPU:1, one launch (start us, length us, event | category | flops | bytes accessed | tf_op | source)
XLA Modules:
  0.0 159.8 jit_solution(17525219402643239957)
XLA Ops:
  0.0 1.3 select_reduce_fusion.table
  1.3 156.0 %attend_all.1 = bf16[32,16,2048]{2,1,0:T(8,128)(2,1)} custom-call(s32[64]{0:T(128)} %select_reduce_fusion.table, s32[32]{0:T(128)} %bitcast.10, bf16[32,16,2048]{2,1,0:T(8,128)(2,1)} %bitcast.6, bf16[4,128,256]{2,1,0:T(8,128)(2,1)} %bitcast.7, bf16[4,128,256]{2,1,0:T(8,128)(2,1)} %bitcast.8, bf16[512,1024]{1,0:T(8,128)(2,1)} %pk.1, bf16[512,1024]{1,0:T(8,128)(2,1)} %pv.1), custom_call_target="tpu_custom_call" | custom-call | tf_op jit(solution)/shard_map/attend_all/pallas_call | solution.py:406
  157.3 2.4 %hand_over.1 = bf16[512,2048]{1,0:T(8,128)(2,1)} custom-call(bf16[512,2048]{1,0:T(8,128)(2,1)} %bitcast.5), custom_call_target="tpu_custom_call" | custom-call | tf_op jit(solution)/shard_map/hand_over/pallas_call | solution.py:448
  (1 shorter events, 0.0 us)

commit v4 on v3

--- a/solution.py
+++ b/solution.py
@@ -45,7 +45,7 @@
 def kernel(
     table, prompt, q_in, ck_in, cv_in, pk, pv, out,
     q, ck, cv, cache, qs, fs, nq, relay_q, fq, no, fo, relay_o, ret0, ret1, own, own_lse,
-    mixed, send_sem, recv_sem, local_sem, load_sem, out_sem,
+    mixed, lse_out, lse_in, send_sem, recv_sem, local_sem, load_sem, out_sem,
 ):
     dp, x = lax.axis_index("dp"), lax.axis_index("mp")
     z, lane = dp // PLANE, dp % PLANE
@@ -148,7 +148,8 @@
     def along(k, src, dst, sign):
         if k < 2:
             return remote([(src, dst, to_z(sign * (1 - 2 * k)))], src, dst)
-        spans = [pl.ds(n * half, half) for n in range(2)]
+        part = src.shape[0] // 2
+        spans = [pl.ds(n * part, part) for n in range(2)]
         return remote(
             [(src.at[span], dst.at[span], to_z(sign * (2 - 4 * n))) for n, span in enumerate(spans)], src, dst
         )
@@ -283,7 +284,25 @@
 
     def pass_far(h, k, copy):
         copy.wait_recv()
-        returned.append(along(k, relay_o.at[h, k], ret[h].at[5 + k], -1))
+        columns = pl.ds(0, SLOT)
+        returned.append(along(k, relay_o.at[h, k, :, :, columns], ret[h].at[5 + k, :, :, columns], -1))
+        lanes_at = lax.broadcasted_iota(jnp.int32, (LEN, HD), 1)
+        for n in range(2):
+            tile = jnp.zeros((LEN, HD), jnp.float32)
+            for i in range(half):
+                tail = relay_o[h, k, n * half + i, :, SLOT:].astype(jnp.float32)
+                tail = jnp.where(lanes_at < 3 * GROUP, tail, 0.0)
+                tile += pltpu.roll(tail, 3 * GROUP * i, 1) if i else tail
+            lse_out[h, k, n] = tile.astype(jnp.bfloat16)
+        returned.append(along(k, lse_out.at[h, k], lse_in.at[h, k], -1))
+
+    def unpack(h):
+        for k in range(3):
+            for n in range(2):
+                tile = lse_in[h, k, n].astype(jnp.float32)
+                for i in range(half):
+                    tail = pltpu.roll(tile, HD - 3 * GROUP * i, 1) if i else tile
+                    ret[h][5 + k, n * half + i, :, SLOT:] = tail.astype(jnp.bfloat16)
 
     def give_near(h, first, last):
         span = pl.ds(first, last - first)
@@ -310,11 +329,11 @@
     back = {k: far(0, k) for k in (2, 0, 1)}
     near(0, 3, 5)
     give_near(0, 3, 5)
+    for copy in edge1:
+        copy.wait_recv()
     for k in (2, 0, 1):
         pass_far(0, k, back[k])
     first = len(returned)
-    for copy in edge1:
-        copy.wait_recv()
     back = {2: far(1, 2), 0: far(1, 0)}
     pass_far(1, 2, back[2])
     back[1] = far(1, 1)
@@ -360,9 +379,11 @@
 
     for copy in returned[:first]:
         copy.wait_recv()
+    unpack(0)
     blend(0)
     for copy in returned[first:]:
         copy.wait_recv()
+    unpack(1)
     blend(1)
     for copy in sent:
         copy.wait_send()
@@ -402,7 +423,7 @@
     blocks = comp_keys.shape[0] // HD
     vmem, smem = pl.BlockSpec(memory_space=pltpu.VMEM), pl.BlockSpec(memory_space=pltpu.SMEM)
     hbm = pl.BlockSpec(memory_space=pl.ANY)
-    copies = 34
+    copies = 40
     out = pl.pallas_call(
         kernel,
         out_shape=jax.ShapeDtypeStruct((comps, LEN, queries.shape[1]), bf16),
@@ -426,6 +447,8 @@
             pltpu.VMEM((comps, LEN, HEADS * SLOT), jnp.float32),
             pltpu.VMEM((comps, HEADS, LEN, HD), jnp.float32),
             pltpu.VMEM((HEADS, comps, LEN, SLOT), bf16),
+            pltpu.VMEM((HEADS, 3, 2, LEN, HD), bf16),
+            pltpu.VMEM((HEADS, 3, 2, LEN, HD), bf16),
             pltpu.SemaphoreType.DMA((copies,)),
             pltpu.SemaphoreType.DMA((copies,)),
             pltpu.SemaphoreType.DMA((4,)),

time: 160 us -> 158 us (0.988)
  Pallas kernels: 158 us -> 156 us
    pallas_call x1, Pallas kernels: 156 us -> 154 us  [body(): pl.pallas_call(kernel, out_shape=jax.ShapeDtypeStruct((comps, LEN, querie...]
where the time goes in v4:
time: 158 us; the launch traced here: 157 us
  Pallas kernels  156 us (99%)
    pallas_call x1, Pallas kernels, body(): pl.pallas_call(kernel, out_shape=jax.ShapeDtypeStruct((comps, LEN, querie...  154 us

profile of v4, /device:TPU:1, one launch (start us, length us, event | category | flops | bytes accessed | tf_op | source)
XLA Modules:
  0.0 157.5 jit_solution(3347569360013271665)
XLA Ops:
  0.0 1.3 select_reduce_fusion.table
  1.3 153.6 %attend_all.1 = bf16[32,16,2048]{2,1,0:T(8,128)(2,1)} custom-call(s32[64]{0:T(128)} %select_reduce_fusion.table, s32[32]{0:T(128)} %bitcast.10, bf16[32,16,2048]{2,1,0:T(8,128)(2,1)} %bitcast.6, bf16[4,128,256]{2,1,0:T(8,128)(2,1)} %bitcast.7, bf16[4,128,256]{2,1,0:T(8,128)(2,1)} %bitcast.8, bf16[512,1024]{1,0:T(8,128)(2,1)} %pk.1, bf16[512,1024]{1,0:T(8,128)(2,1)} %pv.1), custom_call_target="tpu_custom_call" | custom-call | tf_op jit(solution)/shard_map/attend_all/pallas_call | solution.py:427
  154.9 2.4 %hand_over.1 = bf16[512,2048]{1,0:T(8,128)(2,1)} custom-call(bf16[512,2048]{1,0:T(8,128)(2,1)} %bitcast.5), custom_call_target="tpu_custom_call" | custom-call | tf_op jit(solution)/shard_map/hand_over/pallas_call | solution.py:471
  (1 shorter events, 0.0 us)

commit v5 on v4

--- a/solution.py
+++ b/solution.py
@@ -345,15 +345,15 @@
     give_near(1, 4, 5)
 
     def write(h, n):
-        span = pl.ds(n * 4, 4)
+        span = pl.ds(n * 8, 8)
         return pltpu.make_async_copy(
             mixed.at[h, span], out.at[span, :, pl.ds(h * SLOT, SLOT)], out_sem.at[h, n]
         )
 
     def blend(h):
         def step(n, carry):
-            for i in range(4):
-                c = n * 4 + i
+            for i in range(8):
+                c = n * 8 + i
                 distance = (prompt[c] // PLANE - z + RING) % RING
                 place = jnp.where(
                     distance < 3,
@@ -375,7 +375,7 @@
             write(h, n).start()
             return carry
 
-        lax.fori_loop(0, comps // 4, step, 0)
+        lax.fori_loop(0, comps // 8, step, 0)
 
     for copy in returned[:first]:
         copy.wait_recv()
@@ -388,7 +388,7 @@
     for copy in sent:
         copy.wait_send()
     for h in range(HEADS):
-        for n in range(comps // 4):
+        for n in range(comps // 8):
             write(h, n).wait()
 
 
@@ -453,7 +453,7 @@
             pltpu.SemaphoreType.DMA((copies,)),
             pltpu.SemaphoreType.DMA((4,)),
             pltpu.SemaphoreType.DMA((3,)),
-            pltpu.SemaphoreType.DMA((HEADS, comps // 4)),
+            pltpu.SemaphoreType.DMA((HEADS, comps // 8)),
         ],
         compiler_params=pltpu.CompilerParams(
             collective_id=0, has_side_effects=True, vmem_limit_bytes=60 * 1024 * 1024

time: 158 us -> 158 us (level)
  no operation moved by 1% of the time
where the time goes in v5:
time: 158 us; the launch traced here: 157 us
  Pallas kernels  156 us (99%)
    pallas_call x1, Pallas kernels, body(): pl.pallas_call(kernel, out_shape=jax.ShapeDtypeStruct((comps, LEN, querie...  154 us

profile of v5, /device:TPU:1, one launch (start us, length us, event | category | flops | bytes accessed | tf_op | source)
XLA Modules:
  0.0 157.4 jit_solution(3908658599110784788)
XLA Ops:
  0.0 1.3 select_reduce_fusion.table
  1.3 153.5 %attend_all.1 = bf16[32,16,2048]{2,1,0:T(8,128)(2,1)} custom-call(s32[64]{0:T(128)} %select_reduce_fusion.table, s32[32]{0:T(128)} %bitcast.10, bf16[32,16,2048]{2,1,0:T(8,128)(2,1)} %bitcast.6, bf16[4,128,256]{2,1,0:T(8,128)(2,1)} %bitcast.7, bf16[4,128,256]{2,1,0:T(8,128)(2,1)} %bitcast.8, bf16[512,1024]{1,0:T(8,128)(2,1)} %pk.1, bf16[512,1024]{1,0:T(8,128)(2,1)} %pv.1), custom_call_target="tpu_custom_call" | custom-call | tf_op jit(solution)/shard_map/attend_all/pallas_call | solution.py:427
  154.8 2.4 %hand_over.1 = bf16[512,2048]{1,0:T(8,128)(2,1)} custom-call(bf16[512,2048]{1,0:T(8,128)(2,1)} %bitcast.5), custom_call_target="tpu_custom_call" | custom-call | tf_op jit(solution)/shard_map/hand_over/pallas_call | solution.py:471
  (1 shorter events, 0.0 us)
